TPU v7x, 512 devices: a whole 4x4x16 slice. The times are simulated.
512 devices in a mesh: frame: 16 (over x, y_lo, core), clip: 32 (over y_hi, z).
Axes of the slice: x: 4, y: 4 (y_hi: 2, y_lo: 2; y = y_hi * 2 + y_lo), z: 16, core: 2. Of those that a mesh axis runs over, the one named last changes fastest.
Arguments:
- within_frame_asker_matrix: bfloat16 [32, 16, 128, 1536], P('clip', 'frame'), may hold values from -400 to 400
- within_frame_matcher_matrix: bfloat16 [32, 16, 128, 1536], P('clip', 'frame'), may hold values from -6 to 6
- within_frame_payload_matrix: bfloat16 [32, 16, 128, 1536], P('clip', 'frame'), may hold values from -5 to 5
- within_frame_upstream_derivative: bfloat16 [32, 16, 128, 1536], P('clip', 'frame'), may hold values from -48 to 48
- across_time_asker_matrix: bfloat16 [32, 16, 128, 1536], P('clip', 'frame'), may hold values from -400 to 400
- across_time_matcher_matrix: bfloat16 [32, 16, 128, 1536], P('clip', 'frame'), may hold values from -6 to 6
- across_time_payload_matrix: bfloat16 [32, 16, 128, 1536], P('clip', 'frame'), may hold values from -5 to 5
- across_time_upstream_derivative: bfloat16 [32, 16, 128, 1536], P('clip', 'frame'), may hold values from -48 to 48
- sharpness_factor: float32 [2, 12], replicated, may hold values from 0.7 to 1.4
Outputs:
- spatial_query_grad: bfloat16 [32, 16, 128, 1536], P('clip', 'frame')
- spatial_key_grad: bfloat16 [32, 16, 128, 1536], P('clip', 'frame')
- temporal_query_grad: bfloat16 [32, 16, 128, 1536], P('clip', 'frame')
- temporal_key_grad: bfloat16 [32, 16, 128, 1536], P('clip', 'frame')
- temporal_value_grad: bfloat16 [32, 16, 128, 1536], P('clip', 'frame')
- logit_scale_gradient: float32 [2, 12], replicated
All inputs are finite; a program needn't handle non-finite values.
Results may differ from a plain program's by a relative error of at most 0.011.
Values may be sent and summed in bfloat16 or wider, within the bound.
No kernel may reach another device: no remote copies, remote signals or barrier semaphores. Data moves between devices by JAX's collectives and lax.ppermute only.
A program may use at most 64 MiB of HBM per device.

v0:
```python
import math

import jax
import jax.numpy as jnp
from jax import lax
from jax.sharding import PartitionSpec as P


def softmax_mixing_reverse_pass(queries, key_rows, values, cotangent, temper_row, causal):
    head_width = queries.shape[-1]
    raw_scores = jnp.einsum(
        "lbhk,mbhk->bhlm", queries, key_rows, preferred_element_type=jnp.float32
    ) / math.sqrt(head_width)
    scores = temper_row[None, :, None, None] * raw_scores
    if causal:
        length = queries.shape[0]
        row_index = lax.broadcasted_iota(jnp.int32, (length, length), 0)
        col_index = lax.broadcasted_iota(jnp.int32, (length, length), 1)
        scores = jnp.where(col_index <= row_index, scores, -jnp.inf)
    row_max = jnp.max(scores, axis=-1, keepdims=True)
    exponent = jnp.exp(scores - row_max)
    soft_weights = exponent / jnp.sum(exponent, axis=-1, keepdims=True)
    weights_low = soft_weights.astype(jnp.bfloat16)
    value_grad = jnp.einsum(
        "bhlm,lbhk->mbhk", weights_low, cotangent, preferred_element_type=jnp.float32
    )
    weight_grad = jnp.einsum(
        "lbhk,mbhk->bhlm", cotangent, values, preferred_element_type=jnp.float32
    )
    row_delta = jnp.sum(soft_weights * weight_grad, axis=-1, keepdims=True)
    score_grad = soft_weights * (weight_grad - row_delta)
    score_low = score_grad.astype(jnp.bfloat16)
    factor = (temper_row / math.sqrt(head_width))[None, None, :, None]
    query_grad = (
        jnp.einsum("bhlm,mbhk->lbhk", score_low, key_rows, preferred_element_type=jnp.float32)
        * factor
    )
    key_grad = (
        jnp.einsum("bhlm,lbhk->mbhk", score_low, queries, preferred_element_type=jnp.float32)
        * factor
    )
    payload_derivative_share = jnp.sum(score_grad * raw_scores, axis=(2, 3))
    return (
        query_grad.astype(jnp.bfloat16),
        key_grad.astype(jnp.bfloat16),
        value_grad.astype(jnp.bfloat16),
        payload_derivative_share,
    )


def across_time_elements(pieces, temper_row, channel_bundle):
    frames = pieces[0].shape[0]
    count = pieces[0].shape[2]
    features = pieces[0].shape[3]
    shaped = [
        piece.reshape(frames, count, channel_bundle, features // channel_bundle) for piece in pieces
    ]
    grads = softmax_mixing_reverse_pass(
        shaped[0], shaped[1], shaped[2], shaped[3], temper_row, True
    )
    unrolled_vector = tuple((block.reshape(frames, 1, count, features) for block in grads[:3]))
    return (unrolled_vector, grads[3])


def on_device(
    within_frame_asker_matrix,
    within_frame_matcher_matrix,
    within_frame_payload_matrix,
    within_frame_upstream_derivative,
    across_time_asker_matrix,
    across_time_matcher_matrix,
    across_time_payload_matrix,
    across_time_upstream_derivative,
    sharpness_factor,
):
    channel_bundle = sharpness_factor.shape[1]
    patches = within_frame_asker_matrix.shape[2]
    features = within_frame_asker_matrix.shape[3]
    head_width = features // channel_bundle
    groups = lax.axis_size("frame")
    group_width = patches // groups

    def to_heads(block):
        return block.reshape(patches, 1, channel_bundle, head_width)

    def from_heads(block):
        return block.reshape(1, 1, patches, features)

    def to_groups(block):
        return block.reshape(1, groups, group_width, features)

    spatial_result = softmax_mixing_reverse_pass(
        to_heads(within_frame_asker_matrix),
        to_heads(within_frame_matcher_matrix),
        to_heads(within_frame_payload_matrix),
        to_heads(within_frame_upstream_derivative),
        sharpness_factor[0],
        False,
    )
    spatial_part = jnp.sum(spatial_result[3], axis=0)
    incoming_shards = (
        lax.all_to_all(
            to_groups(across_time_asker_matrix), "frame", split_axis=1, concat_axis=0, tiled=True
        ),
        lax.all_to_all(
            to_groups(across_time_matcher_matrix), "frame", split_axis=1, concat_axis=0, tiled=True
        ),
        lax.all_to_all(
            to_groups(across_time_payload_matrix), "frame", split_axis=1, concat_axis=0, tiled=True
        ),
        lax.all_to_all(
            to_groups(across_time_upstream_derivative),
            "frame",
            split_axis=1,
            concat_axis=0,
            tiled=True,
        ),
    )
    unrolled_vector, payload_derivative_share = across_time_elements(
        incoming_shards, sharpness_factor[1], channel_bundle
    )
    temporal_grads = (
        lax.all_to_all(unrolled_vector[0], "frame", split_axis=0, concat_axis=1, tiled=True),
        lax.all_to_all(unrolled_vector[1], "frame", split_axis=0, concat_axis=1, tiled=True),
        lax.all_to_all(unrolled_vector[2], "frame", split_axis=0, concat_axis=1, tiled=True),
    )
    temporal_part = jnp.sum(payload_derivative_share, axis=0)
    scale_norm = 1.0 / math.sqrt(
        lax.axis_size("clip")
        * within_frame_asker_matrix.shape[0]
        * groups
        * within_frame_asker_matrix.shape[1]
        * patches
    )
    summed_totals = lax.psum(jnp.stack([spatial_part, temporal_part]), ("frame", "clip"))
    logit_scale_gradient = summed_totals * scale_norm
    return (
        from_heads(spatial_result[0]),
        from_heads(spatial_result[1]),
        from_heads(temporal_grads[0]),
        from_heads(temporal_grads[1]),
        from_heads(temporal_grads[2]),
        logit_scale_gradient,
    )


def solution(mesh):
    return jax.shard_map(
        on_device,
        mesh=mesh,
        in_specs=(
            P("clip", "frame", None, None),
            P("clip", "frame", None, None),
            P("clip", "frame", None, None),
            P("clip", "frame", None, None),
            P("clip", "frame", None, None),
            P("clip", "frame", None, None),
            P("clip", "frame", None, None),
            P("clip", "frame", None, None),
            P(),
        ),
        out_specs=(
            P("clip", "frame", None, None),
            P("clip", "frame", None, None),
            P("clip", "frame", None, None),
            P("clip", "frame", None, None),
            P("clip", "frame", None, None),
            P(),
        ),
        check_vma=False,
    )
```

profile of v0, /device:TPU:1, one launch (start us, length us, event | category | flops | bytes accessed | tf_op | source)
XLA Modules:
  0.0 206.0 jit_solution(5501737173968254508)
XLA Ops:
  0.6 18.8 %all_to_all.28 = bf16[1,16,8,1536]{3,2,0,1:T(8,128)(2,1)S(1)} all-to-all(bf16[1,16,8,1536]{3,2,0,1:T(8,128)(2,1)} %bitcast.89), channel_id=1, replica_groups=mesh['frame'=16,'clip'=32] {'frame'}, dimensions={1} | all-to-all | bytes 786432 | tf_op jit(solution)/shard_map/all_to_all | solution.py:105
  19.5 4.3 %all-to-all-start = ((bf16[1,16,8,1536]{3,2,0,1:T(8,128)(2,1)}), bf16[1,16,8,1536]{3,2,0,1:T(8,128)(2,1)S(1)}, u32[]{:S(2)}, u32[]{:S(2)}) async-start(bf16[1,16,8,1536]{3,2,0,1:T(8,128)(2,1)} %bitcast.13), calls=%async_computation | async-start | bytes 786432 | tf_op jit(solution)/shard_map/all_to_all | solution.py:102
  25.8 6.6 %all-to-all-done = bf16[1,16,8,1536]{3,2,0,1:T(8,128)(2,1)S(1)} async-done(((bf16[1,16,8,1536]{3,2,0,1:T(8,128)(2,1)}), bf16[1,16,8,1536]{3,2,0,1:T(8,128)(2,1)S(1)}, u32[]{:S(2)}, u32[]{:S(2)}) %all-to-all-start) | async-done | bytes 393248 | tf_op jit(solution)/shard_map/all_to_all | solution.py:102
  32.4 4.7 %all-to-all-start.3 = ((bf16[1,16,8,1536]{3,2,0,1:T(8,128)(2,1)}), bf16[1,16,8,1536]{3,2,0,1:T(8,128)(2,1)}, u32[]{:S(2)}, u32[]{:S(2)}) async-start(bf16[1,16,8,1536]{3,2,0,1:T(8,128)(2,1)} %bitcast.20), calls=%async_computation.3 | async-start | bytes 786432 | tf_op jit(solution)/shard_map/all_to_all | solution.py:108
  37.1 1.5 fusion.43
  39.6 2.0 copy.54
  41.6 2.2 %multiply_reduce_fusion.3 = (f32[12,128]{1,0:T(8,128)S(1)}, f32[12,128,128]{1,2,0:T(8,128)}) fusion(f32[12,128,128]{1,2,0:T(8,128)S(1)} %get-tuple-element.31, f32[12,128]{1,0:T(8,128)S(1)} %get-tuple-element.30, bf16[128,12,128]{0,2,1:T(8,128)(2,1)S(1)} %bitcast.92, bf16[128,12,128]{0,2,1:T(8,128)(2,1)} %bitcast.93), kind=kOutput, calls=%fused_computation.26 | convolution fusion | flops 50919936 | bytes 2371584 | tf_op jit(solution)/shard_map/lbhk,mbhk->bhlm/dot_general | solution.py:27
  43.8 2.1 %all-to-all-done.3 = bf16[1,16,8,1536]{3,2,0,1:T(8,128)(2,1)} async-done(((bf16[1,16,8,1536]{3,2,0,1:T(8,128)(2,1)}), bf16[1,16,8,1536]{3,2,0,1:T(8,128)(2,1)}, u32[]{:S(2)}, u32[]{:S(2)}) %all-to-all-start.3) | async-done | bytes 393248 | tf_op jit(solution)/shard_map/all_to_all | solution.py:108
  45.9 4.1 %all-to-all-start.2 = ((bf16[1,16,8,1536]{3,2,0,1:T(8,128)(2,1)}), bf16[1,16,8,1536]{3,2,0,1:T(8,128)(2,1)S(1)}, u32[]{:S(2)}, u32[]{:S(2)}) async-start(bf16[1,16,8,1536]{3,2,0,1:T(8,128)(2,1)} %bitcast.18), calls=%async_computation.2 | async-start | bytes 786432 | tf_op jit(solution)/shard_map/all_to_all | solution.py:111
  50.6 2.9 %fusion.44 = (f32[8,12,16]{2,1,0:T(8,128)}, f32[8,12,16,16]{2,3,1,0:T(8,128)}) fusion(f32[12]{0:T(128)} %get-tuple-element.28, pred[16,16]{0,1:T(8,128)(4,1)} %iota_compare_fusion, bf16[16,8,12,128]{3,1,2,0:T(8,128)(2,1)S(1)} %bitcast.84, bf16[16,8,12,128]{3,1,2,0:T(8,128)(2,1)S(1)} %bitcast.81), kind=kOutput, calls=%fused_computation.59 | convolution fusion | flops 6389775 | bytes 891184 | tf_op jit(solution)/shard_map/sub | solution.py:21
  53.5 5.1 %all-to-all-done.2 = bf16[1,16,8,1536]{3,2,0,1:T(8,128)(2,1)S(1)} async-done(((bf16[1,16,8,1536]{3,2,0,1:T(8,128)(2,1)}), bf16[1,16,8,1536]{3,2,0,1:T(8,128)(2,1)S(1)}, u32[]{:S(2)}, u32[]{:S(2)}) %all-to-all-start.2) | async-done | bytes 393248 | tf_op jit(solution)/shard_map/all_to_all | solution.py:111
  58.6 1.9 multiply_reduce_fusion.2
  60.6 1.2 multiply_reduce_fusion
  62.8 1.0 copy.121
  63.8 4.1 %all-to-all-start.4 = ((bf16[16,1,8,1536]{3,2,1,0:T(8,128)(2,1)}), bf16[16,1,8,1536]{3,2,1,0:T(8,128)(2,1)S(1)}, u32[]{:S(2)}, u32[]{:S(2)}) async-start(bf16[16,1,8,1536]{3,2,1,0:T(8,128)(2,1)} %bitcast.73), calls=%async_computation.4 | async-start | bytes 786432 | tf_op jit(solution)/shard_map/all_to_all | solution.py:123
  68.0 2.0 multiply_reduce_fusion.1
  70.4 1.0 copy.120
  71.4 5.2 %all-to-all-done.4 = bf16[16,1,8,1536]{3,2,1,0:T(8,128)(2,1)S(1)} async-done(((bf16[16,1,8,1536]{3,2,1,0:T(8,128)(2,1)}), bf16[16,1,8,1536]{3,2,1,0:T(8,128)(2,1)S(1)}, u32[]{:S(2)}, u32[]{:S(2)}) %all-to-all-start.4) | async-done | bytes 393248 | tf_op jit(solution)/shard_map/all_to_all | solution.py:123
  76.6 4.1 %all-to-all-start.5 = ((bf16[16,1,8,1536]{3,2,1,0:T(8,128)(2,1)}), bf16[16,1,8,1536]{3,2,1,0:T(8,128)(2,1)S(1)}, u32[]{:S(2)}, u32[]{:S(2)}) async-start(bf16[16,1,8,1536]{3,2,1,0:T(8,128)(2,1)} %bitcast.72), calls=%async_computation.5 | async-start | bytes 786432 | tf_op jit(solution)/shard_map/all_to_all | solution.py:124
  82.4 1.2 fusion.12
  83.7 1.0 copy.119
  84.7 4.7 %all-to-all-done.5 = bf16[16,1,8,1536]{3,2,1,0:T(8,128)(2,1)S(1)} async-done(((bf16[16,1,8,1536]{3,2,1,0:T(8,128)(2,1)}), bf16[16,1,8,1536]{3,2,1,0:T(8,128)(2,1)S(1)}, u32[]{:S(2)}, u32[]{:S(2)}) %all-to-all-start.5) | async-done | bytes 393248 | tf_op jit(solution)/shard_map/all_to_all | solution.py:124
  89.4 4.1 %all-to-all-start.6 = ((bf16[16,1,8,1536]{3,2,1,0:T(8,128)(2,1)}), bf16[16,1,8,1536]{3,2,1,0:T(8,128)(2,1)S(1)}, u32[]{:S(2)}, u32[]{:S(2)}) async-start(bf16[16,1,8,1536]{3,2,1,0:T(8,128)(2,1)} %bitcast.71), calls=%async_computation.6 | async-start | bytes 786432 | tf_op jit(solution)/shard_map/all_to_all | solution.py:125
  96.4 106.8 %psum.7 = f32[2,12]{1,0:T(2,128)S(1)} all-reduce(f32[2,12]{1,0:T(2,128)S(1)} %pad_maximum_fusion), channel_id=1, replica_groups=mesh['frame'=16,'clip'=32] {'frame','clip'}, use_global_device_ids=true, to_apply=%region_8.9 | all-reduce | flops 24 | bytes 192 | tf_op jit(solution)/shard_map/psum | solution.py:135
  (54 shorter events, 12.3 us)
Async XLA Ops:
  19.5 4.3 %copy-start.13 = (f32[2,12]{1,0:T(2,128)S(1)}, f32[2,12]{1,0:T(2,128)}, u32[]{:S(2)}) copy-start(f32[2,12]{1,0:T(2,128)} %param.17) | copy-start | bytes 292
  19.5 4.8 %copy-start.2 = (bf16[1,1,128,1536]{3,2,1,0:T(8,128)(2,1)S(1)}, bf16[1,1,128,1536]{3,2,1,0:T(8,128)(2,1)}, u32[]{:S(2)}) copy-start(bf16[1,1,128,1536]{3,2,1,0:T(8,128)(2,1)} %param.10) | copy-start | bytes 1179652
  19.5 12.9 %all-to-all-start = ((bf16[1,16,8,1536]{3,2,0,1:T(8,128)(2,1)}), bf16[1,16,8,1536]{3,2,0,1:T(8,128)(2,1)S(1)}, u32[]{:S(2)}, u32[]{:S(2)}) async-start(bf16[1,16,8,1536]{3,2,0,1:T(8,128)(2,1)} %bitcast.13), calls=%async_computation | async-start | bytes 786432 | tf_op jit(solution)/shard_map/all_to_all | solution.py:102
  24.3 12.9 %copy-start.8 = (f32[12]{0:T(128)}, f32[12]{0:T(128)S(1)}, u32[]{:S(2)}) copy-start(f32[12]{0:T(128)S(1)} %get-tuple-element.29) | copy-start | bytes 148
  24.3 1.0 copy-start.3
  32.4 13.5 %all-to-all-start.3 = ((bf16[1,16,8,1536]{3,2,0,1:T(8,128)(2,1)}), bf16[1,16,8,1536]{3,2,0,1:T(8,128)(2,1)}, u32[]{:S(2)}, u32[]{:S(2)}) async-start(bf16[1,16,8,1536]{3,2,0,1:T(8,128)(2,1)} %bitcast.20), calls=%async_computation.3 | async-start | bytes 786432 | tf_op jit(solution)/shard_map/all_to_all | solution.py:108
  37.1 1.5 copy-start.4
  39.6 2.0 copy-start.7
  45.9 12.8 %all-to-all-start.2 = ((bf16[1,16,8,1536]{3,2,0,1:T(8,128)(2,1)}), bf16[1,16,8,1536]{3,2,0,1:T(8,128)(2,1)S(1)}, u32[]{:S(2)}, u32[]{:S(2)}) async-start(bf16[1,16,8,1536]{3,2,0,1:T(8,128)(2,1)} %bitcast.18), calls=%async_computation.2 | async-start | bytes 786432 | tf_op jit(solution)/shard_map/all_to_all | solution.py:111
  58.6 1.9 copy-start.5
  58.6 2.0 copy-start.15
  58.6 2.0 copy-start.17
  61.8 1.0 copy-start
  61.8 0.7 copy-start.10
  63.8 12.8 %all-to-all-start.4 = ((bf16[16,1,8,1536]{3,2,1,0:T(8,128)(2,1)}), bf16[16,1,8,1536]{3,2,1,0:T(8,128)(2,1)S(1)}, u32[]{:S(2)}, u32[]{:S(2)}) async-start(bf16[16,1,8,1536]{3,2,1,0:T(8,128)(2,1)} %bitcast.73), calls=%async_computation.4 | async-start | bytes 786432 | tf_op jit(solution)/shard_map/all_to_all | solution.py:123
  68.0 2.0 copy-start.1
  68.0 2.0 copy-start.11
  76.6 12.8 %all-to-all-start.5 = ((bf16[16,1,8,1536]{3,2,1,0:T(8,128)(2,1)}), bf16[16,1,8,1536]{3,2,1,0:T(8,128)(2,1)S(1)}, u32[]{:S(2)}, u32[]{:S(2)}) async-start(bf16[16,1,8,1536]{3,2,1,0:T(8,128)(2,1)} %bitcast.72), calls=%async_computation.5 | async-start | bytes 786432 | tf_op jit(solution)/shard_map/all_to_all | solution.py:124
  80.7 0.7 copy-start.9
  80.7 1.1 copy-start.16
  81.4 1.1 copy-start.6
  89.4 114.4 %all-to-all-start.6 = ((bf16[16,1,8,1536]{3,2,1,0:T(8,128)(2,1)}), bf16[16,1,8,1536]{3,2,1,0:T(8,128)(2,1)S(1)}, u32[]{:S(2)}, u32[]{:S(2)}) async-start(bf16[16,1,8,1536]{3,2,1,0:T(8,128)(2,1)} %bitcast.71), calls=%async_computation.6 | async-start | bytes 786432 | tf_op jit(solution)/shard_map/all_to_all | solution.py:125
  94.8 0.6 copy-start.12
  94.8 0.6 copy-start.14
where the time goes:
time: 207 us; the launch traced here: 206 us
  blocking collectives  126 us (61%)
  starting transfers between devices  25.5 us (12%)
  waiting for transfers between devices  23.7 us (11%)
  local copies, waits for them, and re-layouts  14 us (7%)
  matrix products  11.1 us (5%)
  other arithmetic  5.22 us (3%)
    psum x1, blocking collectives, on_device(): lax.psum(jnp.stack([spatial_part, temporal_part]), ('frame', 'clip'))  107 us
    all_to_all x1, blocking collectives, on_device(): lax.all_to_all(to_groups(across_time_matcher_matrix), 'frame', split_axis...  18.8 us
    unnamed x45, local copies, waits for them, and re-layouts  10.9 us
    all_to_all x1, waiting for transfers between devices, on_device(): lax.all_to_all(to_groups(across_time_asker_matrix), 'frame', split_axis=1...  6.56 us
    all_to_all x1, waiting for transfers between devices, on_device(): lax.all_to_all(unrolled_vector[0], 'frame', split_axis=0, concat_axis=1,...  5.21 us
    all_to_all x1, waiting for transfers between devices, on_device(): lax.all_to_all(to_groups(across_time_upstream_derivative), 'frame', split...  5.14 us
    all_to_all x1, starting transfers between devices, on_device(): lax.all_to_all(to_groups(across_time_payload_matrix), 'frame', split_axis...  4.74 us
    all_to_all x1, waiting for transfers between devices, on_device(): lax.all_to_all(unrolled_vector[1], 'frame', split_axis=0, concat_axis=1,...  4.7 us
  transfers between devices with their start and end apart: 6, of which 5 were waited for; matrix products, arithmetic and copies ran while one was open for 10% of the time, Pallas kernels for 0%

commit v1 on v0

v1 whole, which is shorter than its diff:
```python
import functools
import math

import jax
import jax.numpy as jnp
from jax import lax
from jax.experimental import pallas as pl
from jax.experimental.pallas import tpu as pltpu
from jax.sharding import PartitionSpec as P

LANES = 128


def dot(a, b, a_dim, b_dim):
    return lax.dot_general(
        a, b, (((a_dim,), (b_dim,)), ((), ())), preferred_element_type=jnp.float32
    )


def head_gradients(queries, keys, values, cotangent, sharpness, allowed):
    inverse_root = 1.0 / math.sqrt(queries.shape[1])
    raw = dot(keys, queries, 1, 1) * inverse_root
    scores = sharpness * raw
    if allowed is not None:
        scores = jnp.where(allowed, scores, -jnp.inf)
    exponent = jnp.exp(scores - jnp.max(scores, axis=0, keepdims=True))
    weights = exponent * (1.0 / jnp.sum(exponent, axis=0, keepdims=True))
    weight_grad = dot(values, cotangent, 1, 1)
    delta = jnp.sum(weights * weight_grad, axis=0, keepdims=True)
    score_grad = weights * (weight_grad - delta)
    share = jnp.sum(jnp.sum(score_grad * raw, axis=0, keepdims=True), axis=1, keepdims=True)
    score_low = score_grad.astype(jnp.bfloat16)
    factor = sharpness * inverse_root
    query_grad = dot(score_low, keys, 0, 0) * factor
    key_grad = dot(score_low, queries, 1, 0) * factor
    return query_grad, key_grad, weights.astype(jnp.bfloat16), share


def spatial_kernel(heads, sharpness_ref, q_ref, k_ref, v_ref, g_ref, dq_ref, dk_ref, share_ref):
    lane = lax.broadcasted_iota(jnp.int32, (1, LANES), 1)
    shares = jnp.zeros((1, LANES), jnp.float32)
    width = q_ref.shape[1] // heads
    for h in range(heads):
        cols = slice(h * width, (h + 1) * width)
        dq, dk, _, share = head_gradients(
            q_ref[:, cols], k_ref[:, cols], v_ref[:, cols], g_ref[:, cols], sharpness_ref[0, h], None
        )
        dq_ref[:, cols] = dq.astype(jnp.bfloat16)
        dk_ref[:, cols] = dk.astype(jnp.bfloat16)
        shares = jnp.where(lane == h, share, shares)
    share_ref[...] = shares


def temporal_kernel(heads, group_width, sharpness_ref, share_ref, x_ref, out_ref):
    rows = x_ref.shape[0]
    features = x_ref.shape[1] // 4
    width = features // heads
    key_row = lax.broadcasted_iota(jnp.int32, (rows, rows), 0)
    query_row = lax.broadcasted_iota(jnp.int32, (rows, rows), 1)
    allowed = (key_row % group_width == query_row % group_width) & (key_row <= query_row)
    lane = lax.broadcasted_iota(jnp.int32, (1, LANES), 1)
    shares = share_ref[...]
    for h in range(heads):
        q, k, v, g = (
            x_ref[:, part * features + h * width : part * features + (h + 1) * width]
            for part in range(4)
        )
        dq, dk, weights_low, share = head_gradients(q, k, v, g, sharpness_ref[1, h], allowed)
        dv = dot(weights_low, g, 1, 0)
        for part, grad in enumerate((dq, dk, dv)):
            start = part * features + h * width
            out_ref[:, start : start + width] = grad.astype(jnp.bfloat16)
        shares = jnp.where(lane == heads + h, share, shares)
    high = shares.astype(jnp.bfloat16).astype(jnp.float32)
    middle = (shares - high).astype(jnp.bfloat16).astype(jnp.float32)
    low = shares - high - middle
    place = lax.broadcasted_iota(jnp.int32, (rows, LANES), 0) % group_width
    pieces = jnp.where(
        place == 0, high, jnp.where(place == 1, middle, jnp.where(place == 2, low, 0.0))
    )
    out_ref[:, 3 * features :] = pieces.astype(jnp.bfloat16)


def kernel_cost(rows, features, heads, dots, arrays):
    return pl.CostEstimate(
        flops=2 * dots * rows * rows * features,
        bytes_accessed=2 * arrays * rows * features,
        transcendentals=heads * rows * rows,
    )


def on_device(sq, sk, sv, sg, tq, tk, tv, tg, sharpness):
    heads = sharpness.shape[1]
    patches, features = sq.shape[2:]
    frames = lax.axis_size("frame")
    clips = lax.axis_size("clip")
    group_width = patches // frames
    rows = frames * group_width
    smem = pl.BlockSpec(memory_space=pltpu.SMEM)
    vmem = pl.BlockSpec(memory_space=pltpu.VMEM)

    sent = jnp.concatenate(
        [a.reshape(frames, group_width, features) for a in (tq, tk, tv, tg)], axis=2
    )
    arrived = lax.all_to_all(sent, "frame", split_axis=0, concat_axis=0, tiled=True)

    spatial_q, spatial_k, shares = pl.pallas_call(
        functools.partial(spatial_kernel, heads),
        out_shape=(
            jax.ShapeDtypeStruct((patches, features), jnp.bfloat16),
            jax.ShapeDtypeStruct((patches, features), jnp.bfloat16),
            jax.ShapeDtypeStruct((1, LANES), jnp.float32),
        ),
        in_specs=[smem, vmem, vmem, vmem, vmem],
        out_specs=(vmem, vmem, vmem),
        cost_estimate=kernel_cost(patches, features, heads, 4, 6),
        name="spatial",
    )(sharpness, *(a.reshape(patches, features) for a in (sq, sk, sv, sg)))

    grads = pl.pallas_call(
        functools.partial(temporal_kernel, heads, group_width),
        out_shape=jax.ShapeDtypeStruct((rows, 3 * features + LANES), jnp.bfloat16),
        in_specs=[smem, vmem, vmem],
        out_specs=vmem,
        cost_estimate=kernel_cost(rows, features, heads, 5, 7),
        name="temporal",
    )(sharpness, shares, arrived.reshape(rows, 4 * features))

    back = lax.all_to_all(
        grads.reshape(frames, group_width, 3 * features + LANES),
        "frame",
        split_axis=0,
        concat_axis=0,
        tiled=True,
    )
    frame_sum = jnp.sum(back[:, :, 3 * features :].astype(jnp.float32), axis=(0, 1))
    everyone = lax.all_to_all(
        jnp.broadcast_to(frame_sum[None, None], (clips, 1, LANES)),
        "clip",
        split_axis=0,
        concat_axis=0,
        tiled=True,
    )
    scale_norm = 1.0 / math.sqrt(clips * sq.shape[0] * frames * sq.shape[1] * patches)
    total = jnp.sum(everyone, axis=(0, 1)) * scale_norm

    def whole(block):
        return block.reshape(1, 1, patches, features)

    return (
        whole(spatial_q),
        whole(spatial_k),
        whole(back[:, :, :features]),
        whole(back[:, :, features : 2 * features]),
        whole(back[:, :, 2 * features : 3 * features]),
        total[: 2 * heads].reshape(2, heads),
    )


def solution(mesh):
    split = P("clip", "frame", None, None)
    return jax.shard_map(
        on_device,
        mesh=mesh,
        in_specs=(split,) * 8 + (P(),),
        out_specs=(split,) * 5 + (P(),),
        check_vma=False,
    )
```

time: 207 us -> 93.6 us (0.45)
  blocking collectives: 126 us -> 22.4 us
  Pallas kernels: 0 us -> 11.6 us
  matrix products: 11.1 us -> 0 us
  local copies, waits for them, and re-layouts: 14 us -> 3.45 us
  waiting for transfers between devices: 23.7 us -> 28 us
  other arithmetic: 5.22 us -> 2.71 us
    psum x1 -> x0, blocking collectives: 107 us -> none  [on_device(): lax.psum(jnp.stack([spatial_part, temporal_part]), ('frame', 'clip'))]
    pallas_call x0 -> x2, Pallas kernels: none -> 11.6 us  [the longest x1 5.88 us: on_device(): pl.pallas_call(functools.partial(spatial_kernel, heads), out_shape=(jax.S...]
    unnamed x45 -> x2, local copies, waits for them, and re-layouts: 10.9 us -> 1.16 us
    dot_general x9 -> x0, matrix products: 8.24 us -> none  [the longest x2 4.13 us: softmax_mixing_reverse_pass(): jnp.einsum('lbhk,mbhk->bhlm', cotangent, values, preferred_element_type=j...]
    all_to_all x6 -> x2, waiting for transfers between devices: 23.7 us -> 28 us  [the longest x1 15.5 us: on_device(): lax.all_to_all(sent, 'frame', split_axis=0, concat_axis=0, tiled=True)]
    all_to_all x1, blocking collectives: 18.8 us -> 22.4 us  [on_device(): lax.all_to_all(grads.reshape(frames, group_width, 3 * features + LANES),...]
    convert_element_type x3 -> x0, local copies, waits for them, and re-layouts: 3.01 us -> none  [the longest x1 1 us: softmax_mixing_reverse_pass(): key_grad.astype(jnp.bfloat16)]
    sub x1 -> x0, matrix products: 2.91 us -> none  [softmax_mixing_reverse_pass(): exponent = jnp.exp(scores - row_max)]
  transfers between devices with their start and end apart: 6 -> 2, of which waited for: 5 -> 2; matrix products, arithmetic and copies ran while one was open for 10% -> 1% of each run, Pallas kernels for 0% -> 6%
where the time goes in v1:
time: 93.6 us; the launch traced here: 93.2 us
  waiting for transfers between devices  28 us (30%)
  starting transfers between devices  24.4 us (26%)
  blocking collectives  22.4 us (24%)
  Pallas kernels  11.6 us (12%)
  local copies, waits for them, and re-layouts  3.45 us (4%)
  other arithmetic  2.71 us (3%)
    all_to_all x1, blocking collectives, on_device(): lax.all_to_all(grads.reshape(frames, group_width, 3 * features + LANES),...  22.4 us
    all_to_all x1, waiting for transfers between devices, on_device(): lax.all_to_all(sent, 'frame', split_axis=0, concat_axis=0, tiled=True)  15.5 us
    all_to_all x1, starting transfers between devices, on_device(): lax.all_to_all(jnp.broadcast_to(frame_sum[None, None], (clips, 1, LANES))...  14 us
    all_to_all x1, waiting for transfers between devices, on_device(): lax.all_to_all(jnp.broadcast_to(frame_sum[None, None], (clips, 1, LANES))...  12.5 us
    all_to_all x1, starting transfers between devices, on_device(): lax.all_to_all(sent, 'frame', split_axis=0, concat_axis=0, tiled=True)  10.4 us
    pallas_call x1, Pallas kernels, on_device(): pl.pallas_call(functools.partial(spatial_kernel, heads), out_shape=(jax.S...  5.88 us
    pallas_call x1, Pallas kernels, on_device(): pl.pallas_call(functools.partial(temporal_kernel, heads, group_width), ou...  5.71 us
    concatenate x1, other arithmetic, on_device(): jnp.concatenate([a.reshape(frames, group_width, features) for a in (tq, t...  2.66 us
  transfers between devices with their start and end apart: 2, of which 2 were waited for; matrix products, arithmetic and copies ran while one was open for 1% of the time, Pallas kernels for 6%

profile of v1, /device:TPU:1, one launch (start us, length us, event | category | flops | bytes accessed | tf_op | source)
XLA Modules:
  0.0 93.2 jit_solution(8779583767028276682)
XLA Ops:
  0.6 2.7 %pad_maximum_fusion = bf16[16,8,6144]{2,1,0:T(8,128)(2,1)} fusion(bf16[16,8,1536]{2,1,0:T(8,128)(2,1)} %bitcast.22, bf16[16,8,1536]{2,1,0:T(8,128)(2,1)} %bitcast.23, bf16[16,8,1536]{2,1,0:T(8,128)(2,1)} %bitcast.24, bf16[16,8,1536]{2,1,0:T(8,128)(2,1)} %bitcast.25), kind=kLoop, calls=%fused_computation | loop fusion | flops 6291456 | bytes 3145728 | tf_op jit(solution)/shard_map/concatenate | solution.py:102
  3.3 10.4 %all-to-all-start = ((bf16[16,8,6144]{2,1,0:T(8,128)(2,1)}), bf16[16,8,6144]{2,1,0:T(8,128)(2,1)S(1)}, u32[]{:S(2)}, u32[]{:S(2)}) async-start(bf16[16,8,6144]{2,1,0:T(8,128)(2,1)} %pad_maximum_fusion), calls=%async_computation | async-start | bytes 3145728 | tf_op jit(solution)/shard_map/all_to_all | solution.py:105
  13.7 5.9 %spatial.1 = (bf16[128,1536]{1,0:T(8,128)(2,1)}, bf16[128,1536]{1,0:T(8,128)(2,1)}, f32[1,128]{1,0:T(1,128)}) custom-call(f32[2,12]{1,0:T(2,128)} %sharpness_ref.3, bf16[128,1536]{1,0:T(8,128)(2,1)} %bitcast.26, bf16[128,1536]{1,0:T(8,128)(2,1)} %bitcast.27, bf16[128,1536]{1,0:T(8,128)(2,1)} %bitcast.28, bf16[128,1536]{1,0:T(8,128)(2,1)} %bitcast.29), custom_call_target="tpu_custom_call" | custom-call | flops 201326592 | bytes 2359296 | tf_op jit(solution)/shard_map/spatial/pallas_call | solution.py:107
  19.5 15.5 %all-to-all-done = bf16[16,8,6144]{2,1,0:T(8,128)(2,1)S(1)} async-done(((bf16[16,8,6144]{2,1,0:T(8,128)(2,1)}), bf16[16,8,6144]{2,1,0:T(8,128)(2,1)S(1)}, u32[]{:S(2)}, u32[]{:S(2)}) %all-to-all-start) | async-done | bytes 1572896 | tf_op jit(solution)/shard_map/all_to_all | solution.py:105
  35.1 0.0 copy-start
  35.1 1.2 %copy-done = bf16[16,8,6144]{2,1,0:T(8,128)(2,1)} copy-done((bf16[16,8,6144]{2,1,0:T(8,128)(2,1)}, bf16[16,8,6144]{2,1,0:T(8,128)(2,1)S(1)}, u32[]{:S(2)}) %copy-start) | copy-done | bytes 1572888
  36.2 5.7 %temporal.1 = bf16[128,4736]{1,0:T(8,128)(2,1)} custom-call(f32[2,12]{1,0:T(2,128)} %sharpness_ref.3, f32[1,128]{1,0:T(1,128)} %get-tuple-element.11.share_ref, bf16[128,6144]{1,0:T(8,128)(2,1)} %bitcast.20), custom_call_target="tpu_custom_call" | custom-call | flops 251658240 | bytes 2752512 | tf_op jit(solution)/shard_map/temporal/pallas_call | solution.py:120
  41.9 22.4 %all_to_all.15 = bf16[16,8,4736]{2,1,0:T(8,128)(2,1)S(1)} all-to-all(bf16[16,8,4736]{2,1,0:T(8,128)(2,1)} %bitcast.21), channel_id=1, replica_groups=mesh['frame'=16,'clip'=32] {'frame'}, dimensions={0} | all-to-all | bytes 2424832 | tf_op jit(solution)/shard_map/all_to_all | solution.py:129
  64.4 0.6 broadcast_in_dim.2
  65.0 14.0 %all-to-all-start.2 = ((f32[32,1,128]{2,1,0:T(1,128)}), f32[32,1,128]{2,1,0:T(1,128)S(1)}, u32[]{:S(2)}, u32[]{:S(2)}) async-start(f32[32,1,128]{2,1,0:T(1,128)} %broadcast_in_dim.2), calls=%async_computation.2 | async-start | bytes 32768 | tf_op jit(solution)/shard_map/all_to_all | solution.py:137
  79.0 1.0 %slice_bitcast_fusion = (bf16[1,1,128,1536]{3,2,1,0:T(8,128)(2,1)}, bf16[1,1,128,1536]{3,2,1,0:T(8,128)(2,1)}, bf16[1,1,128,1536]{3,2,1,0:T(8,128)(2,1)}) fusion(bf16[16,8,4736]{2,1,0:T(8,128)(2,1)S(1)} %all_to_all.15), kind=kLoop, calls=%fused_computation.1 | loop fusion | bytes 2359296 | tf_op jit(solution)/shard_map/reshape | solution.py:148
  80.1 12.5 %all-to-all-done.2 = f32[32,1,128]{2,1,0:T(1,128)S(1)} async-done(((f32[32,1,128]{2,1,0:T(1,128)}), f32[32,1,128]{2,1,0:T(1,128)S(1)}, u32[]{:S(2)}, u32[]{:S(2)}) %all-to-all-start.2) | async-done | bytes 16416 | tf_op jit(solution)/shard_map/all_to_all | solution.py:137
  92.5 0.6 reshape.78
  (3 shorter events, 0.1 us)
Async XLA Ops:
  3.3 31.8 %all-to-all-start = ((bf16[16,8,6144]{2,1,0:T(8,128)(2,1)}), bf16[16,8,6144]{2,1,0:T(8,128)(2,1)S(1)}, u32[]{:S(2)}, u32[]{:S(2)}) async-start(bf16[16,8,6144]{2,1,0:T(8,128)(2,1)} %pad_maximum_fusion), calls=%async_computation | async-start | bytes 3145728 | tf_op jit(solution)/shard_map/all_to_all | solution.py:105
  35.1 1.2 %copy-start = (bf16[16,8,6144]{2,1,0:T(8,128)(2,1)}, bf16[16,8,6144]{2,1,0:T(8,128)(2,1)S(1)}, u32[]{:S(2)}) copy-start(bf16[16,8,6144]{2,1,0:T(8,128)(2,1)S(1)} %all-to-all-done) | copy-start | bytes 4718596
  65.0 27.5 %all-to-all-start.2 = ((f32[32,1,128]{2,1,0:T(1,128)}), f32[32,1,128]{2,1,0:T(1,128)S(1)}, u32[]{:S(2)}, u32[]{:S(2)}) async-start(f32[32,1,128]{2,1,0:T(1,128)} %broadcast_in_dim.2), calls=%async_computation.2 | async-start | bytes 32768 | tf_op jit(solution)/shard_map/all_to_all | solution.py:137

commit v2 on v1

v2 whole, which is shorter than its diff:
```python
import functools
import math

import jax
import jax.numpy as jnp
from jax import lax
from jax.experimental import pallas as pl
from jax.experimental.pallas import tpu as pltpu
from jax.sharding import PartitionSpec as P

LANES = 128
BUNDLE = 12
PACK_PIECES = 4
VMEM_BYTES = 16 * 2**20


def dot(a, b, a_dim, b_dim):
    return lax.dot_general(
        a, b, (((a_dim,), (b_dim,)), ((), ())), preferred_element_type=jnp.float32
    )


def score_gradients(raw, weight_grad, sharpness, allowed):
    scores = sharpness * raw
    if allowed is not None:
        scores = jnp.where(allowed, scores, -jnp.inf)
    exponent = jnp.exp(scores - jnp.max(scores, axis=0, keepdims=True))
    weights = exponent * (1.0 / jnp.sum(exponent, axis=0, keepdims=True))
    delta = jnp.sum(weights * weight_grad, axis=0, keepdims=True)
    score_grad = weights * (weight_grad - delta)
    share = jnp.sum(score_grad * raw, axis=0, keepdims=True)
    return weights, score_grad, share


def bundle_gradients(loads, sharpness, allowed, with_values):
    heads = [load() for load in loads]
    inverse_root = 1.0 / math.sqrt(heads[0][0].shape[1])
    raws = [dot(k, q, 1, 1) for q, k, v, g in heads]
    weight_grads = [dot(v, g, 1, 1) for q, k, v, g in heads]
    parts = [
        score_gradients(raw, weight_grad, sharp * inverse_root, allowed)
        for raw, weight_grad, sharp in zip(raws, weight_grads, sharpness)
    ]
    outs = []
    for (q, k, v, g), (weights, score_grad, share), sharp in zip(heads, parts, sharpness):
        score_low = score_grad.astype(jnp.bfloat16)
        factor = sharp * inverse_root
        grads = [dot(score_low, k, 0, 0) * factor, dot(score_low, q, 1, 0) * factor]
        if with_values:
            grads.append(dot(weights.astype(jnp.bfloat16), g, 1, 0))
        total = jnp.sum(share, axis=1, keepdims=True) * inverse_root
        outs.append(([grad.astype(jnp.bfloat16) for grad in grads], total))
    return outs


def spatial_kernel(heads, sharpness_ref, q_ref, k_ref, v_ref, g_ref, dq_ref, dk_ref, share_ref):
    lane = lax.broadcasted_iota(jnp.int32, (1, LANES), 1)
    shares = jnp.zeros((1, LANES), jnp.float32)
    width = q_ref.shape[1] // heads
    for first in range(0, heads, BUNDLE):
        bundle = range(first, min(first + BUNDLE, heads))
        columns = [slice(h * width, (h + 1) * width) for h in bundle]
        loads = [
            lambda cols=cols: [ref[:, cols] for ref in (q_ref, k_ref, v_ref, g_ref)]
            for cols in columns
        ]
        outs = bundle_gradients(loads, [sharpness_ref[0, h] for h in bundle], None, False)
        for h, cols, ((dq, dk), share) in zip(bundle, columns, outs):
            dq_ref[:, cols] = dq
            dk_ref[:, cols] = dk
            shares = jnp.where(lane == h, share, shares)
    share_ref[...] = shares


def temporal_kernel(heads, group_width, first_frame, sharpness_ref, share_ref, x_ref, out_ref):
    rows = x_ref.shape[0]
    features = x_ref.shape[1] // 4
    width = features // heads
    key_row = lax.broadcasted_iota(jnp.int32, (rows, rows), 0)
    query_row = lax.broadcasted_iota(jnp.int32, (rows, rows), 1)
    key_frame, query_frame = (
        (row // group_width + first_frame) % (rows // group_width) for row in (key_row, query_row)
    )
    allowed = (key_row % group_width == query_row % group_width) & (key_frame <= query_frame)
    lane = lax.broadcasted_iota(jnp.int32, (1, LANES), 1)
    shares = share_ref[...]

    def columns(part, h):
        return slice(part * features + h * width, part * features + (h + 1) * width)

    for first in range(0, heads, BUNDLE):
        bundle = range(first, min(first + BUNDLE, heads))
        loads = [lambda h=h: [x_ref[:, columns(part, h)] for part in range(4)] for h in bundle]
        outs = bundle_gradients(loads, [sharpness_ref[1, h] for h in bundle], allowed, True)
        for h, (grads, share) in zip(bundle, outs):
            for part, grad in enumerate(grads):
                out_ref[:, columns(part, h)] = grad
            shares = jnp.where(lane == heads + h, share, shares)
    high = shares.astype(jnp.bfloat16).astype(jnp.float32)
    middle = (shares - high).astype(jnp.bfloat16).astype(jnp.float32)
    low = shares - high - middle
    place = lax.broadcasted_iota(jnp.int32, (rows, LANES), 0) % group_width
    pieces = jnp.where(
        place == 0, high, jnp.where(place == 1, middle, jnp.where(place == 2, low, 0.0))
    )
    out_ref[:, 3 * features :] = pieces.astype(jnp.bfloat16)


def pack_kernel(q_ref, k_ref, v_ref, g_ref, out_ref, staged_ref, in_sems, out_sems):
    rows, features = q_ref.shape
    step = rows // PACK_PIECES
    pieces = [slice(piece * step, (piece + 1) * step) for piece in range(PACK_PIECES)]
    arriving = [
        [
            pltpu.make_async_copy(
                ref.at[piece],
                staged_ref.at[piece, part * features : (part + 1) * features],
                in_sems.at[part, i],
            )
            for part, ref in enumerate((q_ref, k_ref, v_ref, g_ref))
        ]
        for i, piece in enumerate(pieces)
    ]
    leaving = [
        pltpu.make_async_copy(staged_ref.at[piece], out_ref.at[piece], out_sems.at[i])
        for i, piece in enumerate(pieces)
    ]
    for copies in arriving:
        for copy in copies:
            copy.start()
    for copies, copy_out in zip(arriving, leaving):
        for copy in copies:
            copy.wait()
        copy_out.start()
    for copy_out in leaving:
        copy_out.wait()


def kernel_cost(rows, features, heads, dots, arrays):
    return pl.CostEstimate(
        flops=2 * dots * rows * rows * features,
        bytes_accessed=2 * arrays * rows * features,
        transcendentals=heads * rows * rows,
    )


def on_device(sq, sk, sv, sg, tq, tk, tv, tg, sharpness):
    heads = sharpness.shape[1]
    patches, features = sq.shape[2:]
    frames = lax.axis_size("frame")
    clips = lax.axis_size("clip")
    group_width = patches // frames
    rows = frames * group_width
    first_frame = frames // 2
    frame_groups = [[(i + first_frame) % frames for i in range(frames)]]
    clip_groups = [[(i + 3 * clips // 4) % clips for i in range(clips)]]
    smem = pl.BlockSpec(memory_space=pltpu.SMEM)
    vmem = pl.BlockSpec(memory_space=pltpu.VMEM)

    params = pltpu.CompilerParams(vmem_limit_bytes=VMEM_BYTES)
    hbm = pl.BlockSpec(memory_space=pltpu.HBM)
    sent = pl.pallas_call(
        pack_kernel,
        out_shape=jax.ShapeDtypeStruct((patches, 4 * features), jnp.bfloat16),
        in_specs=[hbm] * 4,
        out_specs=hbm,
        scratch_shapes=[
            pltpu.VMEM((patches, 4 * features), jnp.bfloat16),
            pltpu.SemaphoreType.DMA((4, PACK_PIECES)),
            pltpu.SemaphoreType.DMA((PACK_PIECES,)),
        ],
        cost_estimate=pl.CostEstimate(
            flops=0, bytes_accessed=16 * patches * features, transcendentals=0
        ),
        name="pack",
    )(*(a.reshape(patches, features) for a in (tq, tk, tv, tg)))
    arrived = lax.all_to_all(
        sent.reshape(frames, group_width, 4 * features),
        "frame",
        split_axis=0,
        concat_axis=0,
        axis_index_groups=frame_groups,
        tiled=True,
    )

    spatial_q, spatial_k, shares = pl.pallas_call(
        functools.partial(spatial_kernel, heads),
        out_shape=(
            jax.ShapeDtypeStruct((patches, features), jnp.bfloat16),
            jax.ShapeDtypeStruct((patches, features), jnp.bfloat16),
            jax.ShapeDtypeStruct((1, LANES), jnp.float32),
        ),
        in_specs=[smem, vmem, vmem, vmem, vmem],
        out_specs=(vmem, vmem, vmem),
        compiler_params=params,
        cost_estimate=kernel_cost(patches, features, heads, 4, 6),
        name="spatial",
    )(sharpness, *(a.reshape(patches, features) for a in (sq, sk, sv, sg)))

    grads = pl.pallas_call(
        functools.partial(temporal_kernel, heads, group_width, first_frame),
        out_shape=jax.ShapeDtypeStruct((rows, 3 * features + LANES), jnp.bfloat16),
        in_specs=[smem, vmem, vmem],
        out_specs=vmem,
        compiler_params=params,
        cost_estimate=kernel_cost(rows, features, heads, 5, 7),
        name="temporal",
    )(sharpness, shares, arrived.reshape(rows, 4 * features))

    back = lax.all_to_all(
        grads.reshape(frames, group_width, 3 * features + LANES),
        "frame",
        split_axis=0,
        concat_axis=0,
        axis_index_groups=frame_groups,
        tiled=True,
    )
    frame_sum = jnp.sum(back[:, :, 3 * features :].astype(jnp.float32), axis=(0, 1))
    everyone = lax.all_to_all(
        jnp.broadcast_to(frame_sum[None, None], (clips, 1, LANES)),
        "clip",
        split_axis=0,
        concat_axis=0,
        axis_index_groups=clip_groups,
        tiled=True,
    )
    scale_norm = 1.0 / math.sqrt(clips * sq.shape[0] * frames * sq.shape[1] * patches)
    total = jnp.sum(everyone, axis=(0, 1)) * scale_norm

    def whole(block):
        return block.reshape(1, 1, patches, features)

    return (
        whole(spatial_q),
        whole(spatial_k),
        whole(back[:, :, :features]),
        whole(back[:, :, features : 2 * features]),
        whole(back[:, :, 2 * features : 3 * features]),
        total[: 2 * heads].reshape(2, heads),
    )


def solution(mesh):
    split = P("clip", "frame", None, None)
    return jax.shard_map(
        on_device,
        mesh=mesh,
        in_specs=(split,) * 8 + (P(),),
        out_specs=(split,) * 5 + (P(),),
        check_vma=False,
    )
```

time: 93.6 us -> 78 us (0.83)
  waiting for transfers between devices: 28 us -> 17.1 us
  Pallas kernels: 11.6 us -> 6.54 us
  starting transfers between devices: 24.4 us -> 28.8 us
  other arithmetic: 2.71 us -> 0.06 us
  local copies, waits for them, and re-layouts: 3.45 us -> 2.32 us
    all_to_all x1, waiting for transfers between devices: 12.5 us -> 0.63 us  [on_device(): lax.all_to_all(jnp.broadcast_to(frame_sum[None, None], (clips, 1, LANES))...]
    pallas_call x1, Pallas kernels: 5.88 us -> 2.45 us  [on_device(): pl.pallas_call(functools.partial(spatial_kernel, heads), out_shape=(jax.S...]
    all_to_all x1, starting transfers between devices: 14 us -> 17.3 us  [on_device(): lax.all_to_all(jnp.broadcast_to(frame_sum[None, None], (clips, 1, LANES))...]
    concatenate x1 -> x0, other arithmetic: 2.66 us -> none  [on_device(): jnp.concatenate([a.reshape(frames, group_width, features) for a in (tq, t...]
    pallas_call x1 -> x2, Pallas kernels: 5.71 us -> 4.1 us  [the longest x1 2.41 us: on_device(): pl.pallas_call(pack_kernel, out_shape=jax.ShapeDtypeStruct((patches, 4 *...]
    unnamed x2 -> x10, local copies, waits for them, and re-layouts: 1.16 us -> 0.03 us
    all_to_all x1, starting transfers between devices: 10.4 us -> 11.5 us  [on_device(): lax.all_to_all(sent.reshape(frames, group_width, 4 * features), 'frame',...]
    all_to_all x1, waiting for transfers between devices: 15.5 us -> 16.5 us  [on_device(): lax.all_to_all(sent.reshape(frames, group_width, 4 * features), 'frame',...]
  transfers between devices with their start and end apart: 2 -> 2, of which waited for: 2 -> 2; matrix products, arithmetic and copies ran while one was open for 1% -> 1% of each run, Pallas kernels for 6% -> 3%
where the time goes in v2:
time: 78 us; the launch traced here: 77.3 us
  starting transfers between devices  28.8 us (37%)
  blocking collectives  21.8 us (28%)
  waiting for transfers between devices  17.1 us (22%)
  Pallas kernels  6.54 us (8%)
  local copies, waits for them, and re-layouts  2.32 us (3%)
    all_to_all x1, blocking collectives, on_device(): lax.all_to_all(grads.reshape(frames, group_width, 3 * features + LANES),...  21.8 us
    all_to_all x1, starting transfers between devices, on_device(): lax.all_to_all(jnp.broadcast_to(frame_sum[None, None], (clips, 1, LANES))...  17.3 us
    all_to_all x1, waiting for transfers between devices, on_device(): lax.all_to_all(sent.reshape(frames, group_width, 4 * features), 'frame',...  16.5 us
    all_to_all x1, starting transfers between devices, on_device(): lax.all_to_all(sent.reshape(frames, group_width, 4 * features), 'frame',...  11.5 us
    pallas_call x1, Pallas kernels, on_device(): pl.pallas_call(functools.partial(spatial_kernel, heads), out_shape=(jax.S...  2.45 us
    pallas_call x1, Pallas kernels, on_device(): pl.pallas_call(pack_kernel, out_shape=jax.ShapeDtypeStruct((patches, 4 *...  2.41 us
    pallas_call x1, Pallas kernels, on_device(): pl.pallas_call(functools.partial(temporal_kernel, heads, group_width, fir...  1.68 us
  transfers between devices with their start and end apart: 2, of which 2 were waited for; matrix products, arithmetic and copies ran while one was open for 1% of the time, Pallas kernels for 3%

profile of v2, /device:TPU:1, one launch (start us, length us, event | category | flops | bytes accessed | tf_op | source)
XLA Modules:
  0.0 77.3 jit_solution(12787155298512150705)
XLA Ops:
  0.6 2.4 %pack.1 = bf16[128,6144]{1,0:T(8,128)(2,1)} custom-call(bf16[128,1536]{1,0:T(8,128)(2,1)} %bitcast.28, bf16[128,1536]{1,0:T(8,128)(2,1)} %bitcast.29, bf16[128,1536]{1,0:T(8,128)(2,1)} %bitcast.30, bf16[128,1536]{1,0:T(8,128)(2,1)} %bitcast.31), custom_call_target="tpu_custom_call" | custom-call | bytes 3145728 | tf_op jit(solution)/shard_map/pack/pallas_call | solution.py:162
  3.1 0.0 copy-start
  3.1 0.0 copy-start.1
  3.1 0.0 copy-start.2
  3.1 0.0 copy-start.3
  3.1 0.0 copy-start.4
  3.1 11.5 %all-to-all-start = ((bf16[16,8,6144]{2,1,0:T(8,128)(2,1)}), bf16[16,8,6144]{2,1,0:T(8,128)(2,1)S(1)}, u32[]{:S(2)}, u32[]{:S(2)}) async-start(bf16[16,8,6144]{2,1,0:T(8,128)(2,1)} %bitcast.27), calls=%async_computation | async-start | bytes 3145728 | tf_op jit(solution)/shard_map/all_to_all | solution.py:177
  14.6 0.0 copy-done
  14.6 0.0 copy-done.1
  14.6 0.0 copy-done.2
  14.6 0.0 copy-done.3
  14.6 0.0 copy-done.4
  14.6 2.4 %spatial.1 = (bf16[128,1536]{1,0:T(8,128)(2,1)}, bf16[128,1536]{1,0:T(8,128)(2,1)}, f32[1,128]{1,0:T(1,128)S(1)}) custom-call(f32[2,12]{1,0:T(2,128)S(1)} %copy-done.4, bf16[128,1536]{1,0:T(8,128)(2,1)S(1)} %bitcast.23, bf16[128,1536]{1,0:T(8,128)(2,1)S(1)} %bitcast.24, bf16[128,1536]{1,0:T(8,128)(2,1)S(1)} %bitcast.25, bf16[128,1536]{1,0:T(8,128)(2,1)S(1)} %bitcast.26), custom_call_target="tpu_custom_call" | custom-call | flops 201326592 | bytes 2359296 | tf_op jit(solution)/shard_map/spatial/pallas_call | solution.py:186
  17.1 16.5 %all-to-all-done = bf16[16,8,6144]{2,1,0:T(8,128)(2,1)S(1)} async-done(((bf16[16,8,6144]{2,1,0:T(8,128)(2,1)}), bf16[16,8,6144]{2,1,0:T(8,128)(2,1)S(1)}, u32[]{:S(2)}, u32[]{:S(2)}) %all-to-all-start) | async-done | bytes 1572896 | tf_op jit(solution)/shard_map/all_to_all | solution.py:177
  33.6 1.7 %temporal.1 = bf16[128,4736]{1,0:T(8,128)(2,1)S(1)} custom-call(f32[2,12]{1,0:T(2,128)S(1)} %copy-done.4, f32[1,128]{1,0:T(1,128)S(1)} %get-tuple-element.11.share_ref, bf16[128,6144]{1,0:T(8,128)(2,1)S(1)} %bitcast.21), custom_call_target="tpu_custom_call" | custom-call | flops 251658240 | bytes 2752512 | tf_op jit(solution)/shard_map/temporal/pallas_call | solution.py:200
  35.3 21.8 %all_to_all.15 = bf16[16,8,4736]{2,1,0:T(8,128)(2,1)S(1)} all-to-all(bf16[16,8,4736]{2,1,0:T(8,128)(2,1)S(1)} %bitcast.22), channel_id=1, replica_groups={{256,288,320,352,384,416,448,480,0,32,64,96,128,160,192,224},{257,289,3..., dimensions={0} | all-to-all | bytes 2424832 | tf_op jit(solution)/shard_map/all_to_all | solution.py:210
  57.1 0.6 broadcast_in_dim.2
  57.7 17.3 %all-to-all-start.2 = ((f32[32,1,128]{2,1,0:T(1,128)}), f32[32,1,128]{2,1,0:T(1,128)S(1)}, u32[]{:S(2)}, u32[]{:S(2)}) async-start(f32[32,1,128]{2,1,0:T(1,128)} %broadcast_in_dim.2), calls=%async_computation.2 | async-start | bytes 32768 | tf_op jit(solution)/shard_map/all_to_all | solution.py:219
  75.0 1.0 %slice_bitcast_fusion = (bf16[1,1,128,1536]{3,2,1,0:T(8,128)(2,1)}, bf16[1,1,128,1536]{3,2,1,0:T(8,128)(2,1)}, bf16[1,1,128,1536]{3,2,1,0:T(8,128)(2,1)}) fusion(bf16[16,8,4736]{2,1,0:T(8,128)(2,1)S(1)} %all_to_all.15), kind=kLoop, calls=%fused_computation | loop fusion | bytes 2359296 | tf_op jit(solution)/shard_map/reshape | solution.py:231
  76.0 0.6 all-to-all-done.2
  76.7 0.6 reshape.82
  (3 shorter events, 0.1 us)
Async XLA Ops:
  3.1 11.5 %copy-start = (bf16[1,1,128,1536]{3,2,1,0:T(8,128)(2,1)S(1)}, bf16[1,1,128,1536]{3,2,1,0:T(8,128)(2,1)}, u32[]{:S(2)}) copy-start(bf16[1,1,128,1536]{3,2,1,0:T(8,128)(2,1)} %param.9) | copy-start | bytes 1179652
  3.1 11.5 %copy-start.1 = (bf16[1,1,128,1536]{3,2,1,0:T(8,128)(2,1)S(1)}, bf16[1,1,128,1536]{3,2,1,0:T(8,128)(2,1)}, u32[]{:S(2)}) copy-start(bf16[1,1,128,1536]{3,2,1,0:T(8,128)(2,1)} %param.10) | copy-start | bytes 1179652
  3.1 11.5 %copy-start.2 = (bf16[1,1,128,1536]{3,2,1,0:T(8,128)(2,1)S(1)}, bf16[1,1,128,1536]{3,2,1,0:T(8,128)(2,1)}, u32[]{:S(2)}) copy-start(bf16[1,1,128,1536]{3,2,1,0:T(8,128)(2,1)} %param.11) | copy-start | bytes 1179652
  3.1 11.5 %copy-start.3 = (bf16[1,1,128,1536]{3,2,1,0:T(8,128)(2,1)S(1)}, bf16[1,1,128,1536]{3,2,1,0:T(8,128)(2,1)}, u32[]{:S(2)}) copy-start(bf16[1,1,128,1536]{3,2,1,0:T(8,128)(2,1)} %param.12) | copy-start | bytes 1179652
  3.1 11.5 %copy-start.4 = (f32[2,12]{1,0:T(2,128)S(1)}, f32[2,12]{1,0:T(2,128)}, u32[]{:S(2)}) copy-start(f32[2,12]{1,0:T(2,128)} %sharpness_ref.3) | copy-start | bytes 292
  3.1 30.5 %all-to-all-start = ((bf16[16,8,6144]{2,1,0:T(8,128)(2,1)}), bf16[16,8,6144]{2,1,0:T(8,128)(2,1)S(1)}, u32[]{:S(2)}, u32[]{:S(2)}) async-start(bf16[16,8,6144]{2,1,0:T(8,128)(2,1)} %bitcast.27), calls=%async_computation | async-start | bytes 3145728 | tf_op jit(solution)/shard_map/all_to_all | solution.py:177
  57.7 18.9 %all-to-all-start.2 = ((f32[32,1,128]{2,1,0:T(1,128)}), f32[32,1,128]{2,1,0:T(1,128)S(1)}, u32[]{:S(2)}, u32[]{:S(2)}) async-start(f32[32,1,128]{2,1,0:T(1,128)} %broadcast_in_dim.2), calls=%async_computation.2 | async-start | bytes 32768 | tf_op jit(solution)/shard_map/all_to_all | solution.py:219

commit v3 on v2

--- a/solution.py
+++ b/solution.py
@@ -10,7 +10,6 @@
 
 LANES = 128
 BUNDLE = 12
-PACK_PIECES = 4
 VMEM_BYTES = 16 * 2**20
 
 
@@ -20,10 +19,10 @@
     )
 
 
-def score_gradients(raw, weight_grad, sharpness, allowed):
+def score_gradients(raw, weight_grad, sharpness, hidden):
     scores = sharpness * raw
-    if allowed is not None:
-        scores = jnp.where(allowed, scores, -jnp.inf)
+    if hidden is not None:
+        scores = scores + hidden
     exponent = jnp.exp(scores - jnp.max(scores, axis=0, keepdims=True))
     weights = exponent * (1.0 / jnp.sum(exponent, axis=0, keepdims=True))
     delta = jnp.sum(weights * weight_grad, axis=0, keepdims=True)
@@ -32,13 +31,13 @@
     return weights, score_grad, share
 
 
-def bundle_gradients(loads, sharpness, allowed, with_values):
+def bundle_gradients(loads, sharpness, hidden, with_values):
     heads = [load() for load in loads]
     inverse_root = 1.0 / math.sqrt(heads[0][0].shape[1])
     raws = [dot(k, q, 1, 1) for q, k, v, g in heads]
     weight_grads = [dot(v, g, 1, 1) for q, k, v, g in heads]
     parts = [
-        score_gradients(raw, weight_grad, sharp * inverse_root, allowed)
+        score_gradients(raw, weight_grad, sharp * inverse_root, hidden)
         for raw, weight_grad, sharp in zip(raws, weight_grads, sharpness)
     ]
     outs = []
@@ -82,6 +81,7 @@
         (row // group_width + first_frame) % (rows // group_width) for row in (key_row, query_row)
     )
     allowed = (key_row % group_width == query_row % group_width) & (key_frame <= query_frame)
+    hidden = jnp.where(allowed, 0.0, -jnp.inf)
     lane = lax.broadcasted_iota(jnp.int32, (1, LANES), 1)
     shares = share_ref[...]
 
@@ -91,7 +91,7 @@
     for first in range(0, heads, BUNDLE):
         bundle = range(first, min(first + BUNDLE, heads))
         loads = [lambda h=h: [x_ref[:, columns(part, h)] for part in range(4)] for h in bundle]
-        outs = bundle_gradients(loads, [sharpness_ref[1, h] for h in bundle], allowed, True)
+        outs = bundle_gradients(loads, [sharpness_ref[1, h] for h in bundle], hidden, True)
         for h, (grads, share) in zip(bundle, outs):
             for part, grad in enumerate(grads):
                 out_ref[:, columns(part, h)] = grad
@@ -107,30 +107,23 @@
 
 
 def pack_kernel(q_ref, k_ref, v_ref, g_ref, out_ref, staged_ref, in_sems, out_sems):
-    rows, features = q_ref.shape
-    step = rows // PACK_PIECES
-    pieces = [slice(piece * step, (piece + 1) * step) for piece in range(PACK_PIECES)]
+    features = q_ref.shape[1]
     arriving = [
-        [
-            pltpu.make_async_copy(
-                ref.at[piece],
-                staged_ref.at[piece, part * features : (part + 1) * features],
-                in_sems.at[part, i],
-            )
-            for part, ref in enumerate((q_ref, k_ref, v_ref, g_ref))
-        ]
-        for i, piece in enumerate(pieces)
+        pltpu.make_async_copy(ref, staged_ref.at[part], in_sems.at[part])
+        for part, ref in enumerate((q_ref, k_ref, v_ref, g_ref))
     ]
     leaving = [
-        pltpu.make_async_copy(staged_ref.at[piece], out_ref.at[piece], out_sems.at[i])
-        for i, piece in enumerate(pieces)
-    ]
-    for copies in arriving:
-        for copy in copies:
-            copy.start()
-    for copies, copy_out in zip(arriving, leaving):
-        for copy in copies:
-            copy.wait()
+        pltpu.make_async_copy(
+            staged_ref.at[part],
+            out_ref.at[:, part * features : (part + 1) * features],
+            out_sems.at[part],
+        )
+        for part in range(4)
+    ]
+    for copy in arriving:
+        copy.start()
+    for copy, copy_out in zip(arriving, leaving):
+        copy.wait()
         copy_out.start()
     for copy_out in leaving:
         copy_out.wait()
@@ -153,7 +146,10 @@
     rows = frames * group_width
     first_frame = frames // 2
     frame_groups = [[(i + first_frame) % frames for i in range(frames)]]
-    clip_groups = [[(i + 3 * clips // 4) % clips for i in range(clips)]]
+    clip_order = [(i + 3 * clips // 4) % clips for i in range(clips)]
+    clip_groups = [
+        [(f ^ 2 if c >= clips // 2 else f) * clips + c for c in clip_order] for f in range(frames)
+    ]
     smem = pl.BlockSpec(memory_space=pltpu.SMEM)
     vmem = pl.BlockSpec(memory_space=pltpu.VMEM)
 
@@ -165,9 +161,9 @@
         in_specs=[hbm] * 4,
         out_specs=hbm,
         scratch_shapes=[
-            pltpu.VMEM((patches, 4 * features), jnp.bfloat16),
-            pltpu.SemaphoreType.DMA((4, PACK_PIECES)),
-            pltpu.SemaphoreType.DMA((PACK_PIECES,)),
+            pltpu.VMEM((4, patches, features), jnp.bfloat16),
+            pltpu.SemaphoreType.DMA((4,)),
+            pltpu.SemaphoreType.DMA((4,)),
         ],
         cost_estimate=pl.CostEstimate(
             flops=0, bytes_accessed=16 * patches * features, transcendentals=0
@@ -218,7 +214,7 @@
     frame_sum = jnp.sum(back[:, :, 3 * features :].astype(jnp.float32), axis=(0, 1))
     everyone = lax.all_to_all(
         jnp.broadcast_to(frame_sum[None, None], (clips, 1, LANES)),
-        "clip",
+        ("frame", "clip"),
         split_axis=0,
         concat_axis=0,
         axis_index_groups=clip_groups,

time: 78 us -> 77.3 us (level)
  no operation moved by 1% of the time
where the time goes in v3:
time: 77.3 us; the launch traced here: 76.7 us
  starting transfers between devices  28.2 us (36%)
  blocking collectives  21.8 us (28%)
  waiting for transfers between devices  17.1 us (22%)
  Pallas kernels  6.38 us (8%)
  local copies, waits for them, and re-layouts  2.32 us (3%)
    all_to_all x1, blocking collectives, on_device(): lax.all_to_all(grads.reshape(frames, group_width, 3 * features + LANES),...  21.8 us
    all_to_all x1, starting transfers between devices, on_device(): lax.all_to_all(jnp.broadcast_to(frame_sum[None, None], (clips, 1, LANES))...  16.8 us
    all_to_all x1, waiting for transfers between devices, on_device(): lax.all_to_all(sent.reshape(frames, group_width, 4 * features), 'frame',...  16.5 us
    all_to_all x1, starting transfers between devices, on_device(): lax.all_to_all(sent.reshape(frames, group_width, 4 * features), 'frame',...  11.5 us
    pallas_call x1, Pallas kernels, on_device(): pl.pallas_call(functools.partial(spatial_kernel, heads), out_shape=(jax.S...  2.45 us
    pallas_call x1, Pallas kernels, on_device(): pl.pallas_call(pack_kernel, out_shape=jax.ShapeDtypeStruct((patches, 4 *...  2.25 us
    pallas_call x1, Pallas kernels, on_device(): pl.pallas_call(functools.partial(temporal_kernel, heads, group_width, fir...  1.69 us
  transfers between devices with their start and end apart: 2, of which 2 were waited for; matrix products, arithmetic and copies ran while one was open for 1% of the time, Pallas kernels for 3%

profile of v3, /device:TPU:1, one launch (start us, length us, event | category | flops | bytes accessed | tf_op | source)
XLA Modules:
  0.0 76.7 jit_solution(13120001347533467689)
XLA Ops:
  0.6 2.2 %pack.1 = bf16[128,6144]{1,0:T(8,128)(2,1)} custom-call(bf16[128,1536]{1,0:T(8,128)(2,1)} %bitcast.28, bf16[128,1536]{1,0:T(8,128)(2,1)} %bitcast.29, bf16[128,1536]{1,0:T(8,128)(2,1)} %bitcast.30, bf16[128,1536]{1,0:T(8,128)(2,1)} %bitcast.31), custom_call_target="tpu_custom_call" | custom-call | bytes 3145728 | tf_op jit(solution)/shard_map/pack/pallas_call | solution.py:158
  2.9 0.0 copy-start
  2.9 0.0 copy-start.1
  2.9 0.0 copy-start.2
  2.9 0.0 copy-start.3
  2.9 0.0 copy-start.4
  2.9 11.5 %all-to-all-start = ((bf16[16,8,6144]{2,1,0:T(8,128)(2,1)}), bf16[16,8,6144]{2,1,0:T(8,128)(2,1)S(1)}, u32[]{:S(2)}, u32[]{:S(2)}) async-start(bf16[16,8,6144]{2,1,0:T(8,128)(2,1)} %bitcast.27), calls=%async_computation | async-start | bytes 3145728 | tf_op jit(solution)/shard_map/all_to_all | solution.py:173
  14.4 0.0 copy-done
  14.4 0.0 copy-done.1
  14.4 0.0 copy-done.2
  14.5 0.0 copy-done.3
  14.5 0.0 copy-done.4
  14.5 2.4 %spatial.1 = (bf16[128,1536]{1,0:T(8,128)(2,1)}, bf16[128,1536]{1,0:T(8,128)(2,1)}, f32[1,128]{1,0:T(1,128)S(1)}) custom-call(f32[2,12]{1,0:T(2,128)S(1)} %copy-done.4, bf16[128,1536]{1,0:T(8,128)(2,1)S(1)} %bitcast.23, bf16[128,1536]{1,0:T(8,128)(2,1)S(1)} %bitcast.24, bf16[128,1536]{1,0:T(8,128)(2,1)S(1)} %bitcast.25, bf16[128,1536]{1,0:T(8,128)(2,1)S(1)} %bitcast.26), custom_call_target="tpu_custom_call" | custom-call | flops 201326592 | bytes 2359296 | tf_op jit(solution)/shard_map/spatial/pallas_call | solution.py:182
  16.9 16.5 %all-to-all-done = bf16[16,8,6144]{2,1,0:T(8,128)(2,1)S(1)} async-done(((bf16[16,8,6144]{2,1,0:T(8,128)(2,1)}), bf16[16,8,6144]{2,1,0:T(8,128)(2,1)S(1)}, u32[]{:S(2)}, u32[]{:S(2)}) %all-to-all-start) | async-done | bytes 1572896 | tf_op jit(solution)/shard_map/all_to_all | solution.py:173
  33.4 1.7 %temporal.1 = bf16[128,4736]{1,0:T(8,128)(2,1)S(1)} custom-call(f32[2,12]{1,0:T(2,128)S(1)} %copy-done.4, f32[1,128]{1,0:T(1,128)S(1)} %get-tuple-element.11.share_ref, bf16[128,6144]{1,0:T(8,128)(2,1)S(1)} %bitcast.21), custom_call_target="tpu_custom_call" | custom-call | flops 251658240 | bytes 2752512 | tf_op jit(solution)/shard_map/temporal/pallas_call | solution.py:196
  35.1 21.8 %all_to_all.15 = bf16[16,8,4736]{2,1,0:T(8,128)(2,1)S(1)} all-to-all(bf16[16,8,4736]{2,1,0:T(8,128)(2,1)S(1)} %bitcast.22), channel_id=1, replica_groups={{256,288,320,352,384,416,448,480,0,32,64,96,128,160,192,224},{257,289,3..., dimensions={0} | all-to-all | bytes 2424832 | tf_op jit(solution)/shard_map/all_to_all | solution.py:206
  56.9 0.6 broadcast_in_dim.2
  57.6 16.8 %all-to-all-start.2 = ((f32[32,1,128]{2,1,0:T(1,128)}), f32[32,1,128]{2,1,0:T(1,128)S(1)}, u32[]{:S(2)}, u32[]{:S(2)}) async-start(f32[32,1,128]{2,1,0:T(1,128)} %broadcast_in_dim.2), calls=%async_computation.2 | async-start | bytes 32768 | tf_op jit(solution)/shard_map/all_to_all | solution.py:215
  74.3 1.0 %slice_bitcast_fusion = (bf16[1,1,128,1536]{3,2,1,0:T(8,128)(2,1)}, bf16[1,1,128,1536]{3,2,1,0:T(8,128)(2,1)}, bf16[1,1,128,1536]{3,2,1,0:T(8,128)(2,1)}) fusion(bf16[16,8,4736]{2,1,0:T(8,128)(2,1)S(1)} %all_to_all.15), kind=kLoop, calls=%fused_computation | loop fusion | bytes 2359296 | tf_op jit(solution)/shard_map/reshape | solution.py:227
  75.4 0.6 all-to-all-done.2
  76.0 0.6 reshape.82
  (3 shorter events, 0.1 us)
Async XLA Ops:
  2.9 11.5 %copy-start = (bf16[1,1,128,1536]{3,2,1,0:T(8,128)(2,1)S(1)}, bf16[1,1,128,1536]{3,2,1,0:T(8,128)(2,1)}, u32[]{:S(2)}) copy-start(bf16[1,1,128,1536]{3,2,1,0:T(8,128)(2,1)} %param.9) | copy-start | bytes 1179652
  2.9 11.5 %copy-start.1 = (bf16[1,1,128,1536]{3,2,1,0:T(8,128)(2,1)S(1)}, bf16[1,1,128,1536]{3,2,1,0:T(8,128)(2,1)}, u32[]{:S(2)}) copy-start(bf16[1,1,128,1536]{3,2,1,0:T(8,128)(2,1)} %param.10) | copy-start | bytes 1179652
  2.9 11.5 %copy-start.2 = (bf16[1,1,128,1536]{3,2,1,0:T(8,128)(2,1)S(1)}, bf16[1,1,128,1536]{3,2,1,0:T(8,128)(2,1)}, u32[]{:S(2)}) copy-start(bf16[1,1,128,1536]{3,2,1,0:T(8,128)(2,1)} %param.11) | copy-start | bytes 1179652
  2.9 11.5 %copy-start.3 = (bf16[1,1,128,1536]{3,2,1,0:T(8,128)(2,1)S(1)}, bf16[1,1,128,1536]{3,2,1,0:T(8,128)(2,1)}, u32[]{:S(2)}) copy-start(bf16[1,1,128,1536]{3,2,1,0:T(8,128)(2,1)} %param.12) | copy-start | bytes 1179652
  2.9 11.5 %copy-start.4 = (f32[2,12]{1,0:T(2,128)S(1)}, f32[2,12]{1,0:T(2,128)}, u32[]{:S(2)}) copy-start(f32[2,12]{1,0:T(2,128)} %sharpness_ref.3) | copy-start | bytes 292
  2.9 30.5 %all-to-all-start = ((bf16[16,8,6144]{2,1,0:T(8,128)(2,1)}), bf16[16,8,6144]{2,1,0:T(8,128)(2,1)S(1)}, u32[]{:S(2)}, u32[]{:S(2)}) async-start(bf16[16,8,6144]{2,1,0:T(8,128)(2,1)} %bitcast.27), calls=%async_computation | async-start | bytes 3145728 | tf_op jit(solution)/shard_map/all_to_all | solution.py:173
  57.6 18.4 %all-to-all-start.2 = ((f32[32,1,128]{2,1,0:T(1,128)}), f32[32,1,128]{2,1,0:T(1,128)S(1)}, u32[]{:S(2)}, u32[]{:S(2)}) async-start(f32[32,1,128]{2,1,0:T(1,128)} %broadcast_in_dim.2), calls=%async_computation.2 | async-start | bytes 32768 | tf_op jit(solution)/shard_map/all_to_all | solution.py:215
